TPU v7x, 32 devices: a whole 2x2x4 slice. The times are simulated.
32 devices in a mesh: sub: 8 (over z, y), case: 4 (over x, core).
Axes of the slice: x: 2, y: 2, z: 4, core: 2. Of those that a mesh axis runs over, the one named last changes fastest.
Arguments:
- multipliers: float32 [64, 12288], P('case', 'sub'), may hold values from -6 to 6
- right_side: float32 [64, 12288], P('case', 'sub')
- dual_ops: bfloat16 [12288, 1536], P('sub'), as said below
- glue_match: int32 [8, 2, 128], P('sub'), may hold values from 0 to 127, as said below
- mortar: bfloat16 [8, 4, 128, 128], P('sub'), may hold values from -0.5 to 0.5
- contact_ids: int32 [8, 4], P('sub'), may hold values from 0 to 3
- contact_count: int32 [8], P('sub'), may hold values from 1 to 4
Outputs:
- solved: float32 [64, 12288], P('case', 'sub')
- grad_norm: float32 [1], replicated
Inputs may be any that keep to these rules, and one draw needn't show every extreme that they name: glue_match[s,1] is a permutation of 0 to 127, and glue_match[(s+1) mod 8,0] is its inverse. `dual_ops`: each subdomain's block is symmetric positive definite.
All inputs are finite; a program needn't handle non-finite values.
Results may differ from a plain program's by a relative error of at most 0.002.
Values may be sent and summed in bfloat16 or wider, within the bound.
A program may use at most 64 MiB of HBM per device.

v0:
```python
import functools

import jax
import jax.numpy as jnp
from jax import lax
from jax.experimental import pallas as pl
from jax.experimental.pallas import tpu as pltpu
from jax.sharding import PartitionSpec as P

ITERS = 4
BLK = 128
SLOTS = 4
PENALTY = 0.5
MESH = pl.DeviceIdType.MESH
F32 = jnp.float32
BF16 = jnp.bfloat16


def radices(count):
    out = []
    while count > 1:
        factor = next(f for f in (8, 7, 6, 5, 4, 3, 2, count) if count % f == 0)
        out.append(factor)
        count //= factor
    return out


def halves(value):
    high = value.astype(BF16)
    low = (value - high.astype(F32)).astype(BF16)
    return jnp.concatenate([high, low], axis=0)


def times(value, weight, transposed=False):
    rows = value.shape[0]
    dims = (((1,), (1 if transposed else 0,)), ((), ()))
    both = lax.dot_general(halves(value), weight, dims, preferred_element_type=F32)
    return both[:rows] + both[rows:]


def kernel(
    n, nc, factors, chunks,
    x0_ref, b_ref, k_hbm, match_ref, mortar_ref, ids_ref, count_ref,
    out_ref, norm_ref,
    k_ref, x_ref, g_ref, kx_ref, q_ref, sx_ref, xp_ref, perm_ref, pack_ref, pack_p, mort_p,
    con_send, con_recv, prev_recv, next_recv, sum_send, sum_recv, tot_ref, tot_recv,
    k_sem, ex_send, ex_recv, st_send, st_recv, rel_send, rel_recv, sum_ssem, sum_rsem, tot_ssem, tot_rsem,
):
    rows = x0_ref.shape[0]
    me, cs = lax.axis_index("sub"), lax.axis_index("case")
    nxt, prv, part = lax.rem(me + 1, n), lax.rem(me + n - 1, n), lax.rem(me + n // 2, n)
    depth = k_ref.shape[0] // chunks
    per = SLOTS // nc if SLOTS % nc == 0 else SLOTS
    relayed = per < SLOTS
    contact = pl.ds(2 * BLK, SLOTS * BLK)

    k_copies = [
        pltpu.make_async_copy(
            k_hbm.at[pl.ds(i * depth, depth)], k_ref.at[pl.ds(i * depth, depth)], k_sem.at[i]
        )
        for i in range(chunks)
    ]
    for copy in k_copies:
        copy.start()

    barrier = pltpu.get_barrier_semaphore()
    greeted = 0

    def greet(sub, case):
        pl.semaphore_signal(barrier, inc=1, device_id=(sub, case), device_id_type=MESH)

    stride = 1
    rounds = []
    for f in factors:
        digit = lax.rem(me // stride, f)
        base = me - digit * stride
        rounds.append((f, stride, digit, base))
        for j in range(1, f):
            greet(base + lax.rem(digit + j, f) * stride, cs)
            greeted += 1
        stride *= f
    if len(factors) > 1:
        for other in (nxt, prv, part):
            greet(other, cs)
            greeted += 1
    for j in range(1, nc):
        greet(me, lax.rem(cs + j, nc))
        greeted += 1

    con_send[0] = x0_ref[:, 2 * BLK:(2 + SLOTS) * BLK].astype(BF16)
    line = lax.broadcasted_iota(jnp.int32, (1, BLK), 1) * 0
    for k in range(SLOTS):
        for b in range(SLOTS):
            pack_ref[k * SLOTS + b:k * SLOTS + b + 1, :] = jnp.where(line + ids_ref[0, k] == b, 1.0, 0.0)
        live = SLOTS * SLOTS + k
        pack_ref[live:live + 1, :] = jnp.where(line + count_ref[0] > k, 1.0, 0.0)
    pack_ref[SLOTS * SLOTS + SLOTS:, :] = jnp.zeros((SLOTS, BLK), F32)
    lanes = lax.broadcasted_iota(jnp.int32, (BLK, BLK), 0)
    for side in range(2):
        perm_ref[side] = jnp.where(lanes == match_ref[0, side:side + 1, :], 1.0, 0.0).astype(BF16)

    pl.semaphore_wait(barrier, greeted)

    def remote(src, dst, ssem, rsem, sub, case):
        return pltpu.make_async_remote_copy(
            src_ref=src, dst_ref=dst, send_sem=ssem, recv_sem=rsem,
            device_id=(sub, case), device_id_type=MESH,
        )

    def exchange(vec_ref, slot):
        return [
            remote(con_send.at[slot], con_recv.at[slot], ex_send.at[slot, 0], ex_recv.at[slot, 0], part, cs),
            remote(vec_ref.at[:, pl.ds(BLK, BLK)], prev_recv.at[slot], ex_send.at[slot, 1], ex_recv.at[slot, 1], nxt, cs),
            remote(vec_ref.at[:, pl.ds(0, BLK)], next_recv.at[slot], ex_send.at[slot, 2], ex_recv.at[slot, 2], prv, cs),
        ]

    first = exchange(x0_ref, 0)
    mine = pl.ds(cs * per, per) if relayed else pl.ds(0, SLOTS)
    static = [
        remote(pack_ref, pack_p, st_send.at[0], st_recv.at[0], part, cs),
        remote(mortar_ref.at[0, mine], mort_p.at[mine], st_send.at[1], st_recv.at[1], part, cs),
    ]
    for copy in first + static:
        copy.start()

    x_ref[...] = x0_ref[...]
    for i in range(chunks):
        k_copies[i].wait()
        term = jnp.dot(
            x0_ref[:, i * depth:(i + 1) * depth].astype(BF16), k_ref[i * depth:(i + 1) * depth, :],
            preferred_element_type=F32,
        )
        if i == 0:
            kx_ref[...] = term
        else:
            kx_ref[...] += term

    static[1].wait_recv()
    if relayed:
        relays = []
        for j in range(1, nc):
            copy = remote(mort_p.at[mine], mort_p.at[mine], rel_send.at[j - 1], rel_recv.at[j - 1], me, lax.rem(cs + j, nc))
            copy.start()
            relays.append(copy)

    for copy in first:
        copy.wait()
    static[0].wait()
    sx_ref[0] = times(prev_recv[0], perm_ref[0])
    sx_ref[1] = times(next_recv[0], perm_ref[1])
    xp_ref[...] = con_recv[0].astype(F32)
    static[1].wait_send()
    if relayed:
        for j in range(1, nc):
            from_other = pl.ds(lax.rem(cs + nc - j, nc) * per, per)
            remote(
                mort_p.at[from_other], mort_p.at[from_other], rel_send.at[j - 1], rel_recv.at[j - 1],
                me, lax.rem(cs + j, nc),
            ).wait_recv()
        for copy in relays:
            copy.wait_send()

    row = lax.broadcasted_iota(jnp.int32, (rows, BLK), 0)
    lane = lax.broadcasted_iota(jnp.int32, (rows, BLK), 1)

    def block(value, b):
        return value[:, b * BLK:(b + 1) * BLK]

    def chosen(pack, value, k):
        total = pack[k * SLOTS:k * SLOTS + 1, :] * block(value, 0)
        for b in range(1, SLOTS):
            total += pack[k * SLOTS + b:k * SLOTS + b + 1, :] * block(value, b)
        return total

    def live(pack, k):
        return pack[SLOTS * SLOTS + k:SLOTS * SLOTS + k + 1, :]

    def body(it, carry):
        slot = it + 1
        own, other = pack_ref[...], pack_p[...]
        x, xp = x_ref[:, 2 * BLK:(2 + SLOTS) * BLK], xp_ref[...]
        replies = [jnp.zeros((rows, BLK), F32)] * SLOTS
        for k in range(SLOTS):
            jump_p = (times(chosen(other, x, k), mort_p[k]) - block(xp, k)) * live(other, k)
            back = times(jump_p, mort_p[k], True)
            for b in range(SLOTS):
                replies[b] = replies[b] + other[k * SLOTS + b:k * SLOTS + b + 1, :] * back
        for k in range(SLOTS):
            at = slice((2 + k) * BLK, (3 + k) * BLK)
            jump = (times(chosen(own, xp, k), mortar_ref[0, k]) - block(x, k)) * live(own, k)
            grad = kx_ref[:, at] + (replies[k] - jump) - b_ref[:, at]
            g_ref[:, at] = grad
            con_send[slot, :, k * BLK:(k + 1) * BLK] = grad.astype(BF16)
        for side in range(2):
            at = slice(side * BLK, (side + 1) * BLK)
            g_ref[:, at] = kx_ref[:, at] + PENALTY * (x_ref[:, at] - sx_ref[side]) - b_ref[:, at]
        moved = exchange(g_ref, slot)
        for copy in moved:
            copy.start()
        rest = slice((2 + SLOTS) * BLK, None)
        g_ref[:, rest] = kx_ref[:, rest] - b_ref[:, rest]

        g = g_ref[...]
        q_ref[...] = jnp.dot(g.astype(BF16), k_ref[...], preferred_element_type=F32)
        q = q_ref[...]
        norm = curve = jnp.zeros((rows, BLK), F32)
        for b in range(g.shape[1] // BLK):
            norm += block(g, b) * block(g, b)
            curve += block(g, b) * block(q, b)
        for copy in moved:
            copy.wait()
        sg = [times(prev_recv[slot], perm_ref[0]), times(next_recv[slot], perm_ref[1])]
        for side in range(2):
            curve += PENALTY * block(g, side) * (block(g, side) - sg[side])
        gp = con_recv[slot].astype(F32)
        for k in range(SLOTS):
            image = jnp.dot(chosen(own, gp, k).astype(BF16), mortar_ref[0, k], preferred_element_type=F32)
            jump = (image - block(g, 2 + k)) * live(own, k)
            curve += jump * jump
        norm = jnp.sum(norm, axis=1, keepdims=True)
        curve = jnp.sum(curve, axis=1, keepdims=True)
        packed = jnp.where(lane == row, norm, 0.0) + jnp.where(lane == row + rows, curve, 0.0)
        total = jnp.sum(packed, axis=0, keepdims=True)
        for r, (f, stride, digit, base) in enumerate(rounds):
            sum_send[it, r] = total
            sum_recv[it, r, digit] = total
            sends = []
            for j in range(1, f):
                copy = remote(
                    sum_send.at[it, r], sum_recv.at[it, r, digit], sum_ssem.at[it, r, j], sum_rsem.at[it, r, digit],
                    base + lax.rem(digit + j, f) * stride, cs,
                )
                copy.start()
                sends.append(copy)
            for j in range(1, f):
                source = lax.rem(digit + j, f)
                remote(
                    sum_send.at[it, r], sum_recv.at[it, r, source], sum_ssem.at[it, r, j], sum_rsem.at[it, r, source],
                    base + source * stride, cs,
                ).wait_recv()
            total = sum_recv[it, r, 0]
            for d in range(1, f):
                total = total + sum_recv[it, r, d]
            for copy in sends:
                copy.wait_send()
        tot_ref[...] = total
        wide = jnp.broadcast_to(total, (rows, BLK))
        top = jnp.sum(jnp.where(lane == row, wide, 0.0), axis=1, keepdims=True)
        bottom = jnp.sum(jnp.where(lane == row + rows, wide, 0.0), axis=1, keepdims=True)
        step = top / bottom
        step_wide = jnp.broadcast_to(step, (rows, BLK))

        clipped = []
        for b in range(g.shape[1] // BLK):
            at = slice(b * BLK, (b + 1) * BLK)
            fresh = x_ref[:, at] - step_wide * block(g, b)
            if 2 <= b < 2 + SLOTS:
                kept = jnp.maximum(fresh, 0.0)
                clipped.append((kept - fresh).astype(BF16))
                fresh = kept
            x_ref[:, at] = fresh
        for k in range(SLOTS):
            at = slice(k * BLK, (k + 1) * BLK)
            xp_ref[:, at] = jnp.maximum(xp_ref[:, at] - step_wide * block(gp, k), 0.0)
        for side in range(2):
            sx_ref[side] = sx_ref[side] - step_wide * sg[side]

        @pl.when(it < ITERS - 1)
        def _():
            pushed = jnp.dot(
                jnp.concatenate(clipped, axis=1), k_ref[2 * BLK:(2 + SLOTS) * BLK, :], preferred_element_type=F32
            )
            for b in range(g.shape[1] // BLK):
                at = slice(b * BLK, (b + 1) * BLK)
                kx_ref[:, at] = kx_ref[:, at] - step_wide * q_ref[:, at] + block(pushed, b)

        return carry

    lax.fori_loop(0, ITERS, body, 0)

    tot_recv[cs] = tot_ref[...]
    sends = []
    for j in range(1, nc):
        copy = remote(tot_ref, tot_recv.at[cs], tot_ssem.at[j], tot_rsem.at[cs], me, lax.rem(cs + j, nc))
        copy.start()
        sends.append(copy)
    out_ref[...] = x_ref[...]
    for j in range(1, nc):
        source = lax.rem(cs + j, nc)
        remote(tot_ref, tot_recv.at[source], tot_ssem.at[j], tot_rsem.at[source], me, source).wait_recv()
    for copy in sends:
        copy.wait_send()
    total = tot_recv[0]
    for d in range(1, nc):
        total = total + tot_recv[d]
    flat = lax.broadcasted_iota(jnp.int32, (1, BLK), 1)
    whole = jnp.sum(jnp.where(flat < rows, total, 0.0), axis=1, keepdims=True)
    norm_ref[0] = jnp.sqrt(whole)[0, 0]


def solution(mesh):
    n, nc = mesh.shape["sub"], mesh.shape["case"]
    factors = radices(n)
    chunks = 3

    def on_device(multipliers, right_side, dual_ops, glue_match, mortar, contact_ids, contact_count):
        rows, order = multipliers.shape
        top = max(factors)
        rounds = len(factors)
        vmem = pl.BlockSpec(memory_space=pltpu.VMEM)
        smem = pl.BlockSpec(memory_space=pltpu.SMEM)
        dma = pltpu.SemaphoreType.DMA
        slots = ITERS + 1
        return pl.pallas_call(
            functools.partial(kernel, n, nc, factors, chunks),
            out_shape=(
                jax.ShapeDtypeStruct((rows, order), F32),
                jax.ShapeDtypeStruct((1,), F32),
            ),
            in_specs=[vmem, vmem, pl.BlockSpec(memory_space=pl.ANY), vmem, vmem, smem, smem],
            out_specs=(vmem, smem),
            scratch_shapes=[
                pltpu.VMEM((order, order), BF16),
                pltpu.VMEM((rows, order), F32),
                pltpu.VMEM((rows, order), F32),
                pltpu.VMEM((rows, order), F32),
                pltpu.VMEM((rows, order), F32),
                pltpu.VMEM((2, rows, BLK), F32),
                pltpu.VMEM((rows, SLOTS * BLK), F32),
                pltpu.VMEM((2, BLK, BLK), BF16),
                pltpu.VMEM((SLOTS * SLOTS + 2 * SLOTS, BLK), F32),
                pltpu.VMEM((SLOTS * SLOTS + 2 * SLOTS, BLK), F32),
                pltpu.VMEM((SLOTS, BLK, BLK), BF16),
                pltpu.VMEM((slots, rows, SLOTS * BLK), BF16),
                pltpu.VMEM((slots, rows, SLOTS * BLK), BF16),
                pltpu.VMEM((slots, rows, BLK), F32),
                pltpu.VMEM((slots, rows, BLK), F32),
                pltpu.VMEM((ITERS, rounds, 1, BLK), F32),
                pltpu.VMEM((ITERS, rounds, top, 1, BLK), F32),
                pltpu.VMEM((1, BLK), F32),
                pltpu.VMEM((nc, 1, BLK), F32),
                dma((chunks,)),
                dma((slots, 3)),
                dma((slots, 3)),
                dma((2,)),
                dma((2,)),
                dma((max(nc - 1, 1),)),
                dma((max(nc - 1, 1),)),
                dma((ITERS, rounds, top)),
                dma((ITERS, rounds, top)),
                dma((nc,)),
                dma((nc,)),
            ],
            compiler_params=pltpu.CompilerParams(
                collective_id=0, has_side_effects=True, vmem_limit_bytes=24 * 1024 * 1024
            ),
        )(multipliers, right_side, dual_ops, glue_match, mortar, contact_ids, contact_count)

    in_specs = (
        P("case", "sub"),
        P("case", "sub"),
        P("sub", None),
        P("sub", None, None),
        P("sub", None, None, None),
        P("sub", None),
        P("sub"),
    )
    return jax.shard_map(
        on_device, mesh=mesh, in_specs=in_specs, out_specs=(P("case", "sub"), P()), check_vma=False
    )
```

profile of v0, /device:TPU:0, one launch (start us, length us, event | category | flops | bytes accessed | tf_op | source)
XLA Modules:
  0.0 64.3 jit_solution(14611206265983744309)
XLA Ops:
  1.3 0.0 copy-start
  1.3 2.3 %copy-done = bf16[1536,1536]{1,0:T(8,128)(2,1)S(1)} copy-done((bf16[1536,1536]{1,0:T(8,128)(2,1)S(1)}, bf16[1536,1536]{1,0:T(8,128)(2,1)}, u32[]{:S(2)}) %copy-start) | copy-done | bytes 4718616
  3.6 0.0 copy-start.1
  3.6 0.9 %copy-done.1 = bf16[1,4,128,128]{3,2,1,0:T(8,128)(2,1)S(1)} copy-done((bf16[1,4,128,128]{3,2,1,0:T(8,128)(2,1)S(1)}, bf16[1,4,128,128]{3,2,1,0:T(8,128)(2,1)}, u32[]{:S(2)}) %copy-start.1) | copy-done | bytes 131096
  4.5 0.0 copy-start.2
  4.5 0.9 %copy-done.2 = f32[16,1536]{1,0:T(8,128)S(1)} copy-done((f32[16,1536]{1,0:T(8,128)S(1)}, f32[16,1536]{1,0:T(8,128)}, u32[]{:S(2)}) %copy-start.2) | copy-done | bytes 98328
  5.4 0.0 copy-start.3
  5.4 0.9 %copy-done.3 = f32[16,1536]{1,0:T(8,128)S(1)} copy-done((f32[16,1536]{1,0:T(8,128)S(1)}, f32[16,1536]{1,0:T(8,128)}, u32[]{:S(2)}) %copy-start.3) | copy-done | bytes 98328
  6.3 0.0 copy-start.4
  6.3 0.7 %copy-done.4 = s32[1,2,128]{2,1,0:T(2,128)S(1)} copy-done((s32[1,2,128]{2,1,0:T(2,128)S(1)}, s32[1,2,128]{2,1,0:T(2,128)}, u32[]{:S(2)}) %copy-start.4) | copy-done | bytes 1048
  7.0 0.0 copy-start.5
  7.0 0.7 %copy-done.5 = s32[1,4]{1,0:T(1,128)S(1)} copy-done((s32[1,4]{1,0:T(1,128)S(1)}, s32[1,4]{1,0:T(1,128)}, u32[]{:S(2)}) %copy-start.5) | copy-done | bytes 40
  7.6 54.2 %shard_map.86 = (f32[16,1536]{1,0:T(8,128)S(1)}, f32[1]{0:T(128)}) custom-call(f32[16,1536]{1,0:T(8,128)S(1)} %copy-done.2, f32[16,1536]{1,0:T(8,128)S(1)} %copy-done.3, bf16[1536,1536]{1,0:T(8,128)(2,1)S(1)} %copy-done, s32[1,2,128]{2,1,0:T(2,128)S(1)} %copy-done.4, bf16[1,4,128,128]{3,2,1,0:T(8,128)(2,1)S(1)} %copy-done.1, s32[1,4]{1,0:T(1,128)S(1)} %copy-done.5, ...), custom_call_target="tpu_custom_call" | custom-call | tf_op jit(solution)/shard_map/pallas_call | solution.py:314
  61.9 0.6 copy.12
Async XLA Ops:
  1.3 2.3 %copy-start = (bf16[1536,1536]{1,0:T(8,128)(2,1)S(1)}, bf16[1536,1536]{1,0:T(8,128)(2,1)}, u32[]{:S(2)}) copy-start(bf16[1536,1536]{1,0:T(8,128)(2,1)} %k_hbm.1) | copy-start | bytes 14155780
  3.6 0.9 %copy-start.1 = (bf16[1,4,128,128]{3,2,1,0:T(8,128)(2,1)S(1)}, bf16[1,4,128,128]{3,2,1,0:T(8,128)(2,1)}, u32[]{:S(2)}) copy-start(bf16[1,4,128,128]{3,2,1,0:T(8,128)(2,1)} %mortar_ref.1) | copy-start | bytes 393220
  4.5 0.9 %copy-start.2 = (f32[16,1536]{1,0:T(8,128)S(1)}, f32[16,1536]{1,0:T(8,128)}, u32[]{:S(2)}) copy-start(f32[16,1536]{1,0:T(8,128)} %x0_ref.1) | copy-start | bytes 294916
  5.4 0.9 %copy-start.3 = (f32[16,1536]{1,0:T(8,128)S(1)}, f32[16,1536]{1,0:T(8,128)}, u32[]{:S(2)}) copy-start(f32[16,1536]{1,0:T(8,128)} %b_ref.1) | copy-start | bytes 294916
  6.3 0.7 %copy-start.4 = (s32[1,2,128]{2,1,0:T(2,128)S(1)}, s32[1,2,128]{2,1,0:T(2,128)}, u32[]{:S(2)}) copy-start(s32[1,2,128]{2,1,0:T(2,128)} %match_ref.1) | copy-start | bytes 3076
  7.0 0.7 %copy-start.5 = (s32[1,4]{1,0:T(1,128)S(1)}, s32[1,4]{1,0:T(1,128)}, u32[]{:S(2)}) copy-start(s32[1,4]{1,0:T(1,128)} %ids_ref.1) | copy-start | bytes 52
where the time goes:
time: 64.6 us; the launch traced here: 64.3 us
  Pallas kernels  54.2 us (84%)
  local copies, waits for them, and re-layouts  6.99 us (11%)
  between operations  3.12 us (5%)
    pallas_call x1, Pallas kernels, on_device(): pl.pallas_call(functools.partial(kernel, n, nc, factors, chunks), out_sha...  54.2 us
    unnamed x13, local copies, waits for them, and re-layouts  6.99 us

commit v1 on v0

--- a/solution.py
+++ b/solution.py
@@ -40,11 +40,12 @@
 
 def kernel(
     n, nc, factors, chunks,
-    x0_ref, b_ref, k_hbm, match_ref, mortar_ref, ids_ref, count_ref,
+    x0_hbm, b_hbm, k_hbm, match_hbm, mortar_hbm, ids_hbm, count_hbm,
     out_ref, norm_ref,
+    x0_ref, b_ref, match_ref, mortar_ref, ids_ref, count_ref,
     k_ref, x_ref, g_ref, kx_ref, q_ref, sx_ref, xp_ref, perm_ref, pack_ref, pack_p, mort_p,
     con_send, con_recv, prev_recv, next_recv, sum_send, sum_recv, tot_ref, tot_recv,
-    k_sem, ex_send, ex_recv, st_send, st_recv, rel_send, rel_recv, sum_ssem, sum_rsem, tot_ssem, tot_rsem,
+    in_sem, k_sem, ex_send, ex_recv, st_send, st_recv, rel_send, rel_recv, sum_ssem, sum_rsem, tot_ssem, tot_rsem,
 ):
     rows = x0_ref.shape[0]
     me, cs = lax.axis_index("sub"), lax.axis_index("case")
@@ -60,7 +61,14 @@
         )
         for i in range(chunks)
     ]
-    for copy in k_copies:
+    x0_copy, b_copy, match_copy, mortar_copy, ids_copy, count_copy = loads = [
+        pltpu.make_async_copy(src, dst, in_sem.at[i])
+        for i, (src, dst) in enumerate([
+            (x0_hbm, x0_ref), (b_hbm, b_ref), (match_hbm, match_ref), (mortar_hbm, mortar_ref),
+            (ids_hbm, ids_ref), (count_hbm, count_ref),
+        ])
+    ]
+    for copy in loads + k_copies:
         copy.start()
 
     barrier = pltpu.get_barrier_semaphore()
@@ -87,7 +95,11 @@
         greet(me, lax.rem(cs + j, nc))
         greeted += 1
 
+    x0_copy.wait()
     con_send[0] = x0_ref[:, 2 * BLK:(2 + SLOTS) * BLK].astype(BF16)
+    ids_copy.wait()
+    count_copy.wait()
+    match_copy.wait()
     line = lax.broadcasted_iota(jnp.int32, (1, BLK), 1) * 0
     for k in range(SLOTS):
         for b in range(SLOTS):
@@ -99,6 +111,7 @@
     for side in range(2):
         perm_ref[side] = jnp.where(lanes == match_ref[0, side:side + 1, :], 1.0, 0.0).astype(BF16)
 
+    mortar_copy.wait()
     pl.semaphore_wait(barrier, greeted)
 
     def remote(src, dst, ssem, rsem, sub, case):
@@ -135,6 +148,7 @@
         else:
             kx_ref[...] += term
 
+    b_copy.wait()
     static[1].wait_recv()
     if relayed:
         relays = []
@@ -317,9 +331,15 @@
                 jax.ShapeDtypeStruct((rows, order), F32),
                 jax.ShapeDtypeStruct((1,), F32),
             ),
-            in_specs=[vmem, vmem, pl.BlockSpec(memory_space=pl.ANY), vmem, vmem, smem, smem],
+            in_specs=[pl.BlockSpec(memory_space=pltpu.HBM)] * 7,
             out_specs=(vmem, smem),
             scratch_shapes=[
+                pltpu.VMEM((rows, order), F32),
+                pltpu.VMEM((rows, order), F32),
+                pltpu.VMEM(glue_match.shape, jnp.int32),
+                pltpu.VMEM(mortar.shape, BF16),
+                pltpu.SMEM(contact_ids.shape, jnp.int32),
+                pltpu.SMEM(contact_count.shape, jnp.int32),
                 pltpu.VMEM((order, order), BF16),
                 pltpu.VMEM((rows, order), F32),
                 pltpu.VMEM((rows, order), F32),
@@ -339,6 +359,7 @@
                 pltpu.VMEM((ITERS, rounds, top, 1, BLK), F32),
                 pltpu.VMEM((1, BLK), F32),
                 pltpu.VMEM((nc, 1, BLK), F32),
+                dma((6,)),
                 dma((chunks,)),
                 dma((slots, 3)),
                 dma((slots, 3)),
@@ -352,7 +373,7 @@
                 dma((nc,)),
             ],
             compiler_params=pltpu.CompilerParams(
-                collective_id=0, has_side_effects=True, vmem_limit_bytes=24 * 1024 * 1024
+                collective_id=0, has_side_effects=True, vmem_limit_bytes=58 * 1024 * 1024
             ),
         )(multipliers, right_side, dual_ops, glue_match, mortar, contact_ids, contact_count)
 

time: 64.6 us -> 58.2 us (0.901)
  local copies, waits for them, and re-layouts: 6.99 us -> 1.54 us
  Pallas kernels: 54.2 us -> 53.4 us
    unnamed x13 -> x1, local copies, waits for them, and re-layouts: 6.99 us -> 1.54 us
    pallas_call x1, Pallas kernels: 54.2 us -> 53.4 us  [on_device(): pl.pallas_call(functools.partial(kernel, n, nc, factors, chunks), out_sha...]
where the time goes in v1:
time: 58.2 us; the launch traced here: 58.1 us
  Pallas kernels  53.4 us (92%)
  between operations  3.11 us (5%)
  local copies, waits for them, and re-layouts  1.54 us (3%)
    pallas_call x1, Pallas kernels, on_device(): pl.pallas_call(functools.partial(kernel, n, nc, factors, chunks), out_sha...  53.4 us
    unnamed x1, local copies, waits for them, and re-layouts  1.54 us

profile of v1, /device:TPU:0, one launch (start us, length us, event | category | flops | bytes accessed | tf_op | source)
XLA Modules:
  0.0 58.1 jit_solution(8191825561514058384)
XLA Ops:
  1.3 53.4 %shard_map.86 = (f32[16,1536]{1,0:T(8,128)}, f32[1]{0:T(128)}) custom-call(f32[16,1536]{1,0:T(8,128)} %x0_hbm.1, f32[16,1536]{1,0:T(8,128)} %b_hbm.1, bf16[1536,1536]{1,0:T(8,128)(2,1)} %k_hbm.1, s32[1,2,128]{2,1,0:T(2,128)} %match_hbm.1, bf16[1,4,128,128]{3,2,1,0:T(8,128)(2,1)} %mortar_hbm.1, s32[1,4]{1,0:T(1,128)} %ids_hbm.1, s32[1]{0:T(128)S(6)} %copy.11.count_hbm), custom_call_target="tpu_custom_call" | custom-call | tf_op jit(solution)/shard_map/pallas_call | solution.py:328
  54.7 1.5 %copy.12 = f32[16,1536]{1,0:T(8,128)} copy(f32[16,1536]{1,0:T(8,128)} %get-tuple-element.4) | data formatting | bytes 196608

commit v2 on v1

--- a/solution.py
+++ b/solution.py
@@ -44,8 +44,9 @@
     out_ref, norm_ref,
     x0_ref, b_ref, match_ref, mortar_ref, ids_ref, count_ref,
     k_ref, x_ref, g_ref, kx_ref, q_ref, sx_ref, xp_ref, perm_ref, pack_ref, pack_p, mort_p,
-    con_send, con_recv, prev_recv, next_recv, sum_send, sum_recv, tot_ref, tot_recv,
+    con_send, con_recv, prev_recv, next_recv, cross_ref, mid_perm, mid_tail, mid_head, sum_send, sum_recv, tot_ref, tot_recv,
     in_sem, k_sem, ex_send, ex_recv, st_send, st_recv, rel_send, rel_recv, sum_ssem, sum_rsem, tot_ssem, tot_rsem,
+    mid_send, mid_recv,
 ):
     rows = x0_ref.shape[0]
     me, cs = lax.axis_index("sub"), lax.axis_index("case")
@@ -54,6 +55,10 @@
     per = SLOTS // nc if SLOTS % nc == 0 else SLOTS
     relayed = per < SLOTS
     contact = pl.ds(2 * BLK, SLOTS * BLK)
+
+    halfway = len(factors) == 1 and n >= 4
+    middle, last = n // 2 - 1, n - 1
+    direct = me != 0 if halfway else me >= 0
 
     k_copies = [
         pltpu.make_async_copy(
@@ -136,6 +141,22 @@
     for copy in first + static:
         copy.start()
 
+    def mid_static():
+        return remote(perm_ref.at[0], mid_perm, mid_send.at[0], mid_recv.at[0], middle, cs)
+
+    def mid_first(slot):
+        return remote(g_ref.at[:, pl.ds(0, BLK)], mid_head.at[slot], mid_send.at[1], mid_recv.at[1 + slot], middle, cs)
+
+    def mid_last(slot):
+        return remote(
+            g_ref.at[:, pl.ds(BLK, BLK)], mid_tail.at[slot], mid_send.at[2], mid_recv.at[1 + ITERS + slot], middle, cs
+        )
+
+    if halfway:
+        @pl.when(me == 0)
+        def _():
+            mid_static().start()
+
     x_ref[...] = x0_ref[...]
     for i in range(chunks):
         k_copies[i].wait()
@@ -173,6 +194,19 @@
             ).wait_recv()
         for copy in relays:
             copy.wait_send()
+
+    if halfway:
+        @pl.when(me == 0)
+        def _():
+            mid_static().wait_send()
+
+        @pl.when(me == middle)
+        def _():
+            mid_static_in = pltpu.make_async_remote_copy(
+                src_ref=perm_ref.at[0], dst_ref=mid_perm, send_sem=mid_send.at[0], recv_sem=mid_recv.at[0],
+                device_id=(0, cs), device_id_type=MESH,
+            )
+            mid_static_in.wait_recv()
 
     row = lax.broadcasted_iota(jnp.int32, (rows, BLK), 0)
     lane = lax.broadcasted_iota(jnp.int32, (rows, BLK), 1)
@@ -209,6 +243,14 @@
             at = slice(side * BLK, (side + 1) * BLK)
             g_ref[:, at] = kx_ref[:, at] + PENALTY * (x_ref[:, at] - sx_ref[side]) - b_ref[:, at]
         moved = exchange(g_ref, slot)
+        if halfway:
+            @pl.when(me == 0)
+            def _():
+                mid_first(it).start()
+
+            @pl.when(me == last)
+            def _():
+                mid_last(it).start()
         for copy in moved:
             copy.start()
         rest = slice((2 + SLOTS) * BLK, None)
@@ -221,11 +263,27 @@
         for b in range(g.shape[1] // BLK):
             norm += block(g, b) * block(g, b)
             curve += block(g, b) * block(q, b)
-        for copy in moved:
-            copy.wait()
-        sg = [times(prev_recv[slot], perm_ref[0]), times(next_recv[slot], perm_ref[1])]
         for side in range(2):
-            curve += PENALTY * block(g, side) * (block(g, side) - sg[side])
+            curve += PENALTY * block(g, side) * block(g, side)
+        cross_ref[...] = jnp.zeros((rows, BLK), F32)
+
+        @pl.when(direct)
+        def _():
+            moved[1].wait_recv()
+            cross_ref[...] = g_ref[:, :BLK] * times(prev_recv[slot], perm_ref[0])
+
+        if halfway:
+            @pl.when(me == middle)
+            def _():
+                for sem, dst, sub in ((1 + it, mid_head, 0), (1 + ITERS + it, mid_tail, last)):
+                    pltpu.make_async_remote_copy(
+                        src_ref=g_ref.at[:, pl.ds(0, BLK)], dst_ref=dst.at[it], send_sem=mid_send.at[1],
+                        recv_sem=mid_recv.at[sem], device_id=(sub, cs), device_id_type=MESH,
+                    ).wait_recv()
+                cross_ref[...] += mid_head[it] * times(mid_tail[it], mid_perm[...])
+
+        moved[0].wait_recv()
+        curve = curve - cross_ref[...]
         gp = con_recv[slot].astype(F32)
         for k in range(SLOTS):
             image = jnp.dot(chosen(own, gp, k).astype(BF16), mortar_ref[0, k], preferred_element_type=F32)
@@ -239,7 +297,7 @@
             sum_send[it, r] = total
             sum_recv[it, r, digit] = total
             sends = []
-            for j in range(1, f):
+            for j in sorted(range(1, f), key=lambda j: abs(2 * j - f)):
                 copy = remote(
                     sum_send.at[it, r], sum_recv.at[it, r, digit], sum_ssem.at[it, r, j], sum_rsem.at[it, r, digit],
                     base + lax.rem(digit + j, f) * stride, cs,
@@ -258,6 +316,19 @@
             for copy in sends:
                 copy.wait_send()
         tot_ref[...] = total
+        if halfway:
+            @pl.when(me == 0)
+            def _():
+                moved[1].wait_recv()
+                mid_first(it).wait_send()
+
+            @pl.when(me == last)
+            def _():
+                mid_last(it).wait_send()
+        moved[2].wait_recv()
+        for copy in moved:
+            copy.wait_send()
+        sg = [times(prev_recv[slot], perm_ref[0]), times(next_recv[slot], perm_ref[1])]
         wide = jnp.broadcast_to(total, (rows, BLK))
         top = jnp.sum(jnp.where(lane == row, wide, 0.0), axis=1, keepdims=True)
         bottom = jnp.sum(jnp.where(lane == row + rows, wide, 0.0), axis=1, keepdims=True)
@@ -355,6 +426,10 @@
                 pltpu.VMEM((slots, rows, SLOTS * BLK), BF16),
                 pltpu.VMEM((slots, rows, BLK), F32),
                 pltpu.VMEM((slots, rows, BLK), F32),
+                pltpu.VMEM((rows, BLK), F32),
+                pltpu.VMEM((BLK, BLK), BF16),
+                pltpu.VMEM((ITERS, rows, BLK), F32),
+                pltpu.VMEM((ITERS, rows, BLK), F32),
                 pltpu.VMEM((ITERS, rounds, 1, BLK), F32),
                 pltpu.VMEM((ITERS, rounds, top, 1, BLK), F32),
                 pltpu.VMEM((1, BLK), F32),
@@ -371,6 +446,8 @@
                 dma((ITERS, rounds, top)),
                 dma((nc,)),
                 dma((nc,)),
+                dma((3,)),
+                dma((1 + 2 * ITERS,)),
             ],
             compiler_params=pltpu.CompilerParams(
                 collective_id=0, has_side_effects=True, vmem_limit_bytes=58 * 1024 * 1024

time: 58.2 us -> 53.4 us (0.918)
  Pallas kernels: 53.4 us -> 48.6 us
    pallas_call x1, Pallas kernels: 53.4 us -> 48.6 us  [on_device(): pl.pallas_call(functools.partial(kernel, n, nc, factors, chunks), out_sha...]
where the time goes in v2:
time: 53.4 us; the launch traced here: 53.2 us
  Pallas kernels  48.6 us (91%)
  between operations  3.11 us (6%)
  local copies, waits for them, and re-layouts  1.54 us (3%)
    pallas_call x1, Pallas kernels, on_device(): pl.pallas_call(functools.partial(kernel, n, nc, factors, chunks), out_sha...  48.6 us
    unnamed x1, local copies, waits for them, and re-layouts  1.54 us

profile of v2, /device:TPU:0, one launch (start us, length us, event | category | flops | bytes accessed | tf_op | source)
XLA Modules:
  0.0 53.2 jit_solution(14168568619209178186)
XLA Ops:
  1.3 48.6 %shard_map.86 = (f32[16,1536]{1,0:T(8,128)}, f32[1]{0:T(128)}) custom-call(f32[16,1536]{1,0:T(8,128)} %x0_hbm.1, f32[16,1536]{1,0:T(8,128)} %b_hbm.1, bf16[1536,1536]{1,0:T(8,128)(2,1)} %k_hbm.1, s32[1,2,128]{2,1,0:T(2,128)} %match_hbm.1, bf16[1,4,128,128]{3,2,1,0:T(8,128)(2,1)} %mortar_hbm.1, s32[1,4]{1,0:T(1,128)} %ids_hbm.1, s32[1]{0:T(128)S(6)} %copy.11.count_hbm), custom_call_target="tpu_custom_call" | custom-call | tf_op jit(solution)/shard_map/pallas_call | solution.py:399
  49.9 1.5 %copy.12 = f32[16,1536]{1,0:T(8,128)} copy(f32[16,1536]{1,0:T(8,128)} %get-tuple-element.4) | data formatting | bytes 196608

commit v3 on v2

--- a/solution.py
+++ b/solution.py
@@ -223,6 +223,12 @@
     def live(pack, k):
         return pack[SLOTS * SLOTS + k:SLOTS * SLOTS + k + 1, :]
 
+    def to_cases():
+        return [
+            remote(tot_ref, tot_recv.at[cs], tot_ssem.at[j], tot_rsem.at[cs], me, lax.rem(cs + j, nc))
+            for j in range(1, nc)
+        ]
+
     def body(it, carry):
         slot = it + 1
         own, other = pack_ref[...], pack_p[...]
@@ -239,10 +245,11 @@
             grad = kx_ref[:, at] + (replies[k] - jump) - b_ref[:, at]
             g_ref[:, at] = grad
             con_send[slot, :, k * BLK:(k + 1) * BLK] = grad.astype(BF16)
+        moved = exchange(g_ref, slot)
+        moved[0].start()
         for side in range(2):
             at = slice(side * BLK, (side + 1) * BLK)
             g_ref[:, at] = kx_ref[:, at] + PENALTY * (x_ref[:, at] - sx_ref[side]) - b_ref[:, at]
-        moved = exchange(g_ref, slot)
         if halfway:
             @pl.when(me == 0)
             def _():
@@ -251,8 +258,8 @@
             @pl.when(me == last)
             def _():
                 mid_last(it).start()
-        for copy in moved:
-            copy.start()
+        moved[1].start()
+        moved[2].start()
         rest = slice((2 + SLOTS) * BLK, None)
         g_ref[:, rest] = kx_ref[:, rest] - b_ref[:, rest]
 
@@ -316,6 +323,12 @@
             for copy in sends:
                 copy.wait_send()
         tot_ref[...] = total
+
+        @pl.when(it == ITERS - 1)
+        def _():
+            for copy in to_cases():
+                copy.start()
+
         if halfway:
             @pl.when(me == 0)
             def _():
@@ -364,11 +377,7 @@
     lax.fori_loop(0, ITERS, body, 0)
 
     tot_recv[cs] = tot_ref[...]
-    sends = []
-    for j in range(1, nc):
-        copy = remote(tot_ref, tot_recv.at[cs], tot_ssem.at[j], tot_rsem.at[cs], me, lax.rem(cs + j, nc))
-        copy.start()
-        sends.append(copy)
+    sends = to_cases()
     out_ref[...] = x_ref[...]
     for j in range(1, nc):
         source = lax.rem(cs + j, nc)

time: 53.4 us -> 53.5 us (level)
  no operation moved by 1% of the time
where the time goes in v3:
time: 53.5 us; the launch traced here: 53.3 us
  Pallas kernels  48.6 us (91%)
  between operations  3.11 us (6%)
  local copies, waits for them, and re-layouts  1.54 us (3%)
    pallas_call x1, Pallas kernels, on_device(): pl.pallas_call(functools.partial(kernel, n, nc, factors, chunks), out_sha...  48.6 us
    unnamed x1, local copies, waits for them, and re-layouts  1.54 us

profile of v3, /device:TPU:0, one launch (start us, length us, event | category | flops | bytes accessed | tf_op | source)
XLA Modules:
  0.0 53.3 jit_solution(14791040460468039655)
XLA Ops:
  1.3 48.6 %shard_map.86 = (f32[16,1536]{1,0:T(8,128)}, f32[1]{0:T(128)}) custom-call(f32[16,1536]{1,0:T(8,128)} %x0_hbm.1, f32[16,1536]{1,0:T(8,128)} %b_hbm.1, bf16[1536,1536]{1,0:T(8,128)(2,1)} %k_hbm.1, s32[1,2,128]{2,1,0:T(2,128)} %match_hbm.1, bf16[1,4,128,128]{3,2,1,0:T(8,128)(2,1)} %mortar_hbm.1, s32[1,4]{1,0:T(1,128)} %ids_hbm.1, s32[1]{0:T(128)S(6)} %copy.11.count_hbm), custom_call_target="tpu_custom_call" | custom-call | tf_op jit(solution)/shard_map/pallas_call | solution.py:408
  49.9 1.5 %copy.12 = f32[16,1536]{1,0:T(8,128)} copy(f32[16,1536]{1,0:T(8,128)} %get-tuple-element.4) | data formatting | bytes 196608
